TPU v7x, 32 devices: a whole 2x2x4 slice. The times are simulated.
32 devices in a mesh: section: 4 (over z), req: 4 (over y, x), tp: 2 (over core).
Axes of the slice: x: 2, y: 2, z: 4, core: 2. Of those that a mesh axis runs over, the one named last changes fastest.
Arguments:
- hidden: bfloat16 [4, 4, 64, 8192], P(None, 'section', 'req', 'tp'), may hold values from -6 to 6
- norm_gain: bfloat16 [4, 8192], P('section', 'tp'), may hold values from 0.099609375 to 1.8984375
- w_kv: bfloat16 [4, 8192, 2, 1024], P('section', None, None, 'tp'), may hold values from -0.0625 to 0.0625
- queries: bfloat16 [4, 4, 64, 8192], P(None, 'section', 'req', 'tp'), may hold values from -120 to 120
- cache_kv: bfloat16 [4, 64, 2, 128, 1024], P('section', 'req', None, None, 'tp'), may hold values from -4 to 4
- exits: int32 [4, 64], P(None, 'req'), may hold values from 0 to 4, as said below
- lengths: int32 [64], P('req'), may hold values from 2 to 124, as said below
Outputs:
- attn_out: bfloat16 [4, 4, 64, 8192], P(None, 'section', 'req', 'tp')
- new_kv: bfloat16 [4, 4, 64, 2, 1024], P(None, 'section', 'req', None, 'tp')
Inputs may be any that keep to these rules, and one draw needn't show every extreme that they name: `exits`: in each step, among the 16 requests of each aligned block, no layer below 4 is named by more than 2 requests, some layer below 4 is named by exactly 2, and some request names 4. `lengths`: every aligned block of 16 requests holds a request of length 124.
All inputs are finite; a program needn't handle non-finite values.
Results may differ from a plain program's by a relative error of at most 0.0056.
Values may be sent and summed in bfloat16 or wider, within the bound.
A program may use at most 128 MiB of HBM per device.

v0:
```python
import jax
import jax.numpy as jnp
from jax import lax
from jax.sharding import PartitionSpec as P

D = 8192
HEAD = 128
EXIT_CAP = 2


EPSILON = 1e-05
ROPE_BASE = 500000.0


def apply_rotary(key_heads, positions):
    half_width = key_heads.shape[-1] // 2
    exponent = jnp.arange(half_width, dtype=jnp.float32) * (2.0 / key_heads.shape[-1])
    frequency = ROPE_BASE ** (-exponent)
    angles = positions.astype(jnp.float32)[..., None, None] * frequency
    cosine = jnp.cos(angles)
    sine_part = jnp.sin(angles)
    lower = key_heads[..., :half_width]
    upper = key_heads[..., half_width:]
    return jnp.concatenate(
        [lower * cosine - upper * sine_part, upper * cosine + lower * sine_part], axis=-1
    )


def local(hidden, norm_gain, w_kv, queries, cache_kv, exits, lengths):
    num_steps = hidden.shape[0]
    local_reqs = hidden.shape[2]
    section_index = lax.axis_index("section")
    own_rows = hidden[:, 0]
    leaving = exits == section_index
    same_exit = exits[:, :, None] == exits[:, None, :]
    req_order = jnp.arange(local_reqs, dtype=jnp.int32)
    earlier_req = req_order[None, :] < req_order[:, None]
    slot_rank = jnp.sum((same_exit & earlier_req[None]).astype(jnp.int32), axis=-1)
    slot_index = jnp.arange(EXIT_CAP, dtype=jnp.int32)
    pick_table = (
        leaving[:, None, :] & (slot_rank[:, None, :] == slot_index[None, :, None])
    ).astype(jnp.bfloat16)
    packed = jnp.einsum(
        "tcr,trd->tcd", pick_table, own_rows, preferred_element_type=jnp.float32
    ).astype(jnp.bfloat16)
    every_exit = lax.all_gather(packed, "section", axis=1, tiled=True)
    wanted = exits * EXIT_CAP + slot_rank
    columns = jnp.arange(every_exit.shape[1], dtype=jnp.int32)
    chooser = (wanted[:, :, None] == columns[None, None, :]).astype(jnp.bfloat16)
    arrived = jnp.einsum(
        "trs,tsd->trd", chooser, every_exit, preferred_element_type=jnp.float32
    ).astype(jnp.bfloat16)
    source_rows = jnp.where((exits < section_index)[..., None], arrived, own_rows)
    flat_count = num_steps * local_reqs
    rows_float = source_rows.astype(jnp.float32)
    squares = lax.psum(jnp.sum(rows_float * rows_float, axis=-1), "tp")
    inverse = lax.rsqrt(squares / D + EPSILON)
    normed_part = (rows_float * inverse[..., None] * norm_gain[0].astype(jnp.float32)).astype(
        jnp.bfloat16
    )
    normed_part = normed_part.reshape(flat_count, normed_part.shape[-1])
    normed = lax.all_gather(normed_part, "tp", axis=1, tiled=True)
    kv_local = w_kv.shape[-1]
    flat_weight = w_kv[0].reshape(w_kv.shape[1], 2 * kv_local)
    kv_pairs = jnp.dot(normed, flat_weight, preferred_element_type=jnp.float32)
    local_heads = kv_local // HEAD
    kv_pairs = kv_pairs.reshape(num_steps, local_reqs, 2, local_heads, HEAD)
    positions = lengths[None, :] + jnp.arange(num_steps, dtype=jnp.int32)[:, None]
    new_keys = apply_rotary(kv_pairs[:, :, 0], positions).astype(jnp.bfloat16)
    new_values = kv_pairs[:, :, 1].astype(jnp.bfloat16)
    fresh_kv = jnp.stack([new_keys, new_values], axis=2).reshape(num_steps, local_reqs, 2, kv_local)
    kv_cache = cache_kv[0]
    cache_len = kv_cache.shape[2]
    slot_ids = jnp.arange(cache_len, dtype=jnp.int32)
    for step_index in range(num_steps):
        written = slot_ids[None, :] == positions[step_index][:, None]
        kv_cache = jnp.where(
            written[:, None, :, None], fresh_kv[step_index][:, :, None, :], kv_cache
        )
    all_keys = kv_cache[:, 0].reshape(local_reqs, cache_len, local_heads, HEAD)
    all_values = kv_cache[:, 1].reshape(local_reqs, cache_len, local_heads, HEAD)
    groups = queries.shape[-1] // kv_local
    query_heads = queries[:, 0].reshape(num_steps, local_reqs, local_heads, groups, HEAD)
    scores = jnp.einsum(
        "trkgd,rckd->trkgc", query_heads, all_keys, preferred_element_type=jnp.float32
    ) * HEAD ** (-0.5)
    visible = slot_ids[None, None, :] <= positions[:, :, None]
    scores = jnp.where(visible[:, :, None, None, :], scores, -1e30)
    top_score = jnp.max(scores, axis=-1, keepdims=True)
    weights = jnp.exp(scores - top_score)
    weights = (weights / jnp.sum(weights, axis=-1, keepdims=True)).astype(jnp.bfloat16)
    attended = jnp.einsum(
        "trkgc,rckd->trkgd", weights, all_values, preferred_element_type=jnp.float32
    )
    live_mask = (section_index < exits).astype(jnp.float32)
    attended = attended * live_mask[:, :, None, None, None]
    attended = attended.reshape(num_steps, 1, local_reqs, queries.shape[-1]).astype(jnp.bfloat16)
    return (attended, fresh_kv[:, None])


def solution(mesh):
    placed = (
        P(None, "section", "req", "tp"),
        P("section", "tp"),
        P("section", None, None, "tp"),
        P(None, "section", "req", "tp"),
        P("section", "req", None, None, "tp"),
        P(None, "req"),
        P("req"),
    )
    return jax.shard_map(
        local,
        mesh=mesh,
        in_specs=placed,
        out_specs=(P(None, "section", "req", "tp"), P(None, "section", "req", None, "tp")),
        check_vma=False,
    )
```

profile of v0, /device:TPU:0, one launch (start us, length us, event | category | flops | bytes accessed | tf_op | source)
XLA Modules:
  0.0 114.1 jit_solution(13396211766782370707)
XLA Ops:
  7.2 0.0 copy-start.1
  7.2 0.0 all-gather.2.cloned.1.call-start
  7.2 0.7 compare_convert_fusion
  7.9 1.0 convert_reduce_fusion
  8.9 0.7 multiply_add_fusion
  9.6 1.3 %convolution_convert_fusion.1 = bf16[4,2,4096]{2,1,0:T(2,128)(2,1)S(1)} fusion(bf16[4,1,16,4096]{3,2,1,0:T(8,128)(2,1)} %param.7, pred[4,16]{1,0:T(4,128)(4,1)S(1)} %get-tuple-element.20, s32[4,16]{1,0:T(4,128)S(1)} %convert_reduce_fusion), kind=kOutput, calls=%fused_computation.4 | convolution fusion | flops 1081600 | bytes 590144 | tf_op jit(solution)/shard_map/tcr,trd->tcd/dot_general | solution.py:43
  10.8 0.1 copy.53
  10.9 15.6 %all_gather.6 = bf16[4,8,4096]{2,0,1:T(4,128)(2,1)S(1)} all-gather(bf16[4,2,4096]{2,0,1:T(4,128)(2,1)S(1)} %copy.53), channel_id=1, replica_groups=mesh['section'=4,'req'=4,'tp'=2] {'section'}, dimensions={1}, use_global_device_ids=true | all-gather | bytes 327680 | tf_op jit(solution)/shard_map/all_gather | solution.py:46
  26.5 1.6 %multiply_reduce_fusion = (f32[4,16]{1,0:T(4,128)S(1)}, f32[4,16,4096]{2,1,0:T(8,128)S(1)}) fusion(bf16[4,1,16,4096]{3,2,1,0:T(8,128)(2,1)} %param.7, bf16[4,8,4096]{2,0,1:T(4,128)(2,1)S(1)} %all_gather.6, s32[4,16]{1,0:T(4,128)S(1)} %multiply_add_fusion, pred[4,16]{1,0:T(4,128)(4,1)S(1)} %get-tuple-element.19), kind=kOutput, calls=%fused_computation.19 | convolution fusion | flops 5505472 | bytes 1835584 | tf_op jit(solution)/shard_map/trs,tsd->trd/dot_general | solution.py:50
  28.1 2.5 %psum.7 = f32[4,16]{1,0:T(4,128)S(1)} all-reduce(f32[4,16]{1,0:T(4,128)S(1)} %get-tuple-element.27), channel_id=1, replica_groups=mesh['section'=4,'req'=4,'tp'=2] {'tp'}, use_global_device_ids=true, to_apply=%region_2.3 | all-reduce | flops 64 | bytes 512 | tf_op jit(solution)/shard_map/psum | solution.py:56
  30.6 0.7 convert_element_type.90
  31.3 1.0 multiply_convert_fusion
  32.3 0.0 all-gather.2.cloned.1.call-update
  32.3 0.0 copy-done.1
  32.3 0.1 copy.63
  32.4 16.7 %copy.81 = bf16[1024,8,2,512]{3,1,2,0:T(8,128)(2,1)} copy(bf16[1024,8,2,512]{3,2,1,0:T(2,128)(2,1)} %bitcast.92) | data formatting | bytes 33554432
  49.1 21.0 %copy.55 = bf16[1024,8192]{1,0:T(8,128)(2,1)} copy(bf16[1024,8192]{0,1:T(8,128)(2,1)} %bitcast.91) | data formatting | bytes 33554432 | tf_op jit(solution)/shard_map/dot_general | solution.py:65
  70.1 0.0 copy-start
  70.1 6.3 %copy.62 = bf16[1,16,2,128,512]{3,4,1,2,0:T(8,128)(2,1)} copy(bf16[1,16,2,128,512]{4,3,2,1,0:T(8,128)(2,1)} %param.11) | data formatting | bytes 8388608 | tf_op args[4]
  76.4 0.0 copy-done
  76.4 0.1 copy.82
  76.5 0.1 copy.67
  76.6 0.1 iota_compare_fusion.3
  76.6 0.1 iota_compare_fusion.5
  76.7 0.1 iota_compare_fusion
  76.8 0.2 multiply_cosine_fusion
  77.0 0.0 all-gather.2.cloned.1.call-done
  77.0 9.0 %fusion.30 = f32[4,16,2,4,128]{4,1,3,2,0:T(8,128)S(1)} fusion(bf16[4,16,8192,1,1]{2,1,4,3,0:T(8,128)(2,1)} %bitcast.101, bf16[2,4,128,8192,1]{3,2,1,0,4:T(8,128)(2,1)} %bitcast.93), kind=kOutput, calls=%fused_computation.70 | convolution fusion | flops 1073741824 | bytes 18087936 | tf_op jit(solution)/shard_map/dot_general | solution.py:65
  86.0 0.1 subtract_bitcast_fusion
  86.2 0.1 maximum_convert_fusion
  86.5 11.1 %fusion.5 = bf16[16,2,128,512]{2,3,0,1:T(8,128)(2,1)S(1)} fusion(bf16[1,16,2,128,512]{3,4,1,2,0:T(8,128)(2,1)} %copy.62, pred[16,128]{1,0:T(8,128)(4,1)S(1)} %get-tuple-element.31, pred[16,128]{1,0:T(8,128)(4,1)S(1)} %get-tuple-element.32, pred[16,128]{1,0:T(8,128)(4,1)S(1)} %get-tuple-element.33, pred[16,128]{1,0:T(8,128)(4,1)S(1)} %get-tuple-element.34, ...), kind=kLoop, calls=%fused_computation.8 | loop fusion | flops 8388608 | bytes 8527872 | tf_op jit(solution)/shard_map/jit(_where)/select_n | solution.py:77
  97.7 1.7 %fusion.26 = (bf16[16,1,128,512]{2,3,0,1:T(8,128)(2,1)}, bf16[16,1,128,512]{2,3,0,1:T(8,128)(2,1)S(1)}) fusion(bf16[16,2,128,512]{2,3,0,1:T(8,128)(2,1)S(1)} %fusion.5), kind=kLoop, calls=%fused_computation.68 | loop fusion | bytes 8388608 | tf_op jit(solution)/shard_map/slice | solution.py:80
  99.4 3.4 %fusion.27 = (f32[4,16,4,8]{3,0,2,1:T(4,128)S(1)}, f32[4,16,4,8,128]{4,3,0,2,1:T(8,128)}) fusion(bf16[16,128,4,128,1]{1,3,4,2,0:T(8,128)(2,1)} %bitcast.96, bf16[4,16,4,8,128]{4,3,2,1,0:T(8,128)(2,1)S(1)} %bitcast.98, pred[4,16,128]{2,0,1:T(4,128)(4,1)S(1)} %iota_compare_fusion), kind=kOutput, calls=%fused_computation.69 | convolution fusion | flops 68157568 | bytes 3686400 | tf_op jit(solution)/shard_map/sub | solution.py:90
  102.8 2.5 %fusion.11 = bf16[4,16,4,8,128]{4,3,0,2,1:T(8,128)(2,1)S(1)} fusion(bf16[16,128,4,128,1]{1,3,4,2,0:T(8,128)(2,1)S(1)} %bitcast.95, f32[4,16,4,8,128]{4,3,0,2,1:T(8,128)} %get-tuple-element.30, f32[4,16]{0,1:T(8,128)S(1)} %copy.67, f32[4,16,4,8]{3,0,2,1:T(4,128)S(1)} %get-tuple-element.29), kind=kOutput, calls=%fused_computation.16 | convolution fusion | flops 68157440 | bytes 3678464 | tf_op jit(solution)/shard_map/trkgc,rckd->trkgd/dot_general | solution.py:92
  105.2 0.1 copy.68
  105.3 1.0 convert_element_type.88
  106.4 0.8 copy.72
  (21 shorter events, 0.3 us)
Async XLA Ops:
  7.2 25.1 %copy-start.1 = (s32[16]{0:T(128)S(1)}, s32[16]{0:T(128)}, u32[]{:S(2)}) copy-start(s32[16]{0:T(128)} %param.13) | copy-start | bytes 196
  7.2 69.9 %all-gather.2.cloned.1.call-start = ((), (), s32[]{:S(2)}) async-start(), calls=%async_computation | async-start | bytes 1572864 | tf_op jit(solution)/shard_map/all_gather | solution.py:62
  70.1 6.3 %copy-start = (bf16[4,1,16,4096]{3,2,1,0:T(8,128)(2,1)S(1)}, bf16[4,1,16,4096]{3,2,1,0:T(8,128)(2,1)}, u32[]{:S(2)}) copy-start(bf16[4,1,16,4096]{3,2,1,0:T(8,128)(2,1)} %param.10) | copy-start | bytes 1572868
Sparse Core Ops, SparseCore 0:
  32.4 10.5 all-gather.1
where the time goes:
time: 115 us; the launch traced here: 114 us
  local copies, waits for them, and re-layouts  48.2 us (42%)
  blocking collectives  18.1 us (16%)
  matrix products  17.6 us (15%)
  other arithmetic  15.8 us (14%)
  between operations  14.3 us (12%)
    unnamed x8, local copies, waits for them, and re-layouts  23.8 us
    dot_general x1, local copies, waits for them, and re-layouts, local(): kv_pairs = jnp.dot(normed, flat_weight, preferred_element_type=jnp.float32)  21 us
    all_gather x1, blocking collectives, local(): every_exit = lax.all_gather(packed, 'section', axis=1, tiled=True)  15.6 us
    select_n x1, other arithmetic, local(): jnp.where(written[:, None, :, None], fresh_kv[step_index][:, :, None, :],...  11.1 us
    dot_general x1, matrix products, local(): kv_pairs = jnp.dot(normed, flat_weight, preferred_element_type=jnp.float32)  8.96 us
    sub x1, matrix products, local(): weights = jnp.exp(scores - top_score)  3.38 us
    dot_general x1, matrix products, local(): jnp.einsum('trkgc,rckd->trkgd', weights, all_values, preferred_element_ty...  2.46 us
    psum x1, blocking collectives, local(): squares = lax.psum(jnp.sum(rows_float * rows_float, axis=-1), 'tp')  2.45 us
  transfers between devices with their start and end apart: 1, of which 0 were waited for; matrix products, arithmetic and copies ran while one was open for 39% of the time, Pallas kernels for 0%

commit v1 on v0

v1 whole, which is shorter than its diff:
```python
import functools
import math

import jax
import jax.numpy as jnp
from jax import lax
from jax.experimental import pallas as pl
from jax.experimental.pallas import tpu as pltpu
from jax.sharding import PartitionSpec as P

HEAD = 128
EXIT_CAP = 2
EPSILON = 1e-05
ROPE_BASE = 500000.0
CHUNKS = 4
BF = jnp.bfloat16
F32 = jnp.float32
MESH = pl.DeviceIdType.MESH


def iota(shape, axis):
    return lax.broadcasted_iota(jnp.int32, shape, axis)


def kernel(S, TP, hid, gain, w_hbm, q_hbm, c_hbm, ecol, erow, pos, lens,
           out, kvout,
           wv, cv, qv, qs, os, ms, ls, xf, gb, pack, gsend, gfull, lk, acc,
           wsem, csem, qsem, sec_send, sec_recv, x_send, x_recv, g_send, g_recv, f_send, f_recv):
    T, R, Dl = hid.shape
    D, _, N = w_hbm.shape
    nt = N // HEAD
    M = T * R
    half = Dl // 2
    rows = T * EXIT_CAP
    slot = 2 * rows
    C = c_hbm.shape[2]
    HG = qs.shape[2]
    G = HG // nt
    sec = lax.axis_index("section")
    req = lax.axis_index("req")
    tp = lax.axis_index("tp")

    barrier = pltpu.get_barrier_semaphore()
    for d in range(1, S):
        pl.semaphore_signal(barrier, inc=1, device_id=(lax.rem(sec + d, S), req, tp), device_id_type=MESH)
    for d in range(1, TP):
        pl.semaphore_signal(barrier, inc=1, device_id=(sec, req, lax.rem(tp + d, TP)), device_id_type=MESH)

    q_copy = pltpu.make_async_copy(q_hbm, qv, qsem)
    q_copy.start()
    c_copies = [pltpu.make_async_copy(c_hbm.at[pl.ds(i * (R // 2), R // 2)], cv.at[pl.ds(i * (R // 2), R // 2)], csem.at[i])
                for i in range(2)]
    for c in c_copies:
        c.start()
    cd = D // CHUNKS

    def w_copy(c, n):
        return pltpu.make_async_copy(
            w_hbm.at[pl.ds(c * cd, cd), :, pl.ds(n * HEAD, HEAD)],
            wv.at[n, pl.ds(c * cd, cd)], wsem.at[c, n])

    for c in range(CHUNKS):
        for n in range(nt):
            w_copy(c, n).start()

    ec = ecol[...]
    er = erow[...]
    ri, rj = iota((M, M), 0), iota((M, M), 1)
    same = (ec == er) & (ri // R == rj // R)
    rank_row = jnp.sum((same & (ri < rj)).astype(F32), axis=0, keepdims=True).astype(jnp.int32)
    rank_col = jnp.sum((same & (rj < ri)).astype(F32), axis=1, keepdims=True).astype(jnp.int32)
    pk, pj = iota((rows, M), 0), iota((rows, M), 1)
    pick = ((er == sec) & (pk == (pj // R) * EXIT_CAP + rank_row)).astype(F32).astype(BF)
    hv = hid[...].reshape(M, Dl)
    packed = jnp.dot(pick, hv, preferred_element_type=F32)
    pack[...] = jnp.concatenate([packed[:, :half], packed[:, half:]], axis=0).astype(BF)
    gsend[...] = jnp.broadcast_to(gain[...].astype(F32), gsend.shape)
    pl.semaphore_wait(barrier, S - 1 + TP - 1)

    def sec_copy(d, src, target):
        return pltpu.make_async_remote_copy(
            src_ref=pack, dst_ref=gb.at[tp, pl.ds(src * slot, slot)],
            send_sem=sec_send.at[d - 1], recv_sem=sec_recv.at[d - 1],
            device_id=(target, req, tp), device_id_type=MESH)

    for d in range(1, S):
        @pl.when(sec + d < S)
        def _():
            sec_copy(d, sec, lax.rem(sec + d, S)).start()

    def x_copy(d):
        return pltpu.make_async_remote_copy(
            src_ref=hid, dst_ref=xf.at[tp], send_sem=x_send.at[d - 1], recv_sem=x_recv.at[d - 1],
            device_id=(sec, req, lax.rem(tp + d, TP)), device_id_type=MESH)

    def g_copy(d):
        return pltpu.make_async_remote_copy(
            src_ref=gsend, dst_ref=gfull.at[tp], send_sem=g_send.at[d - 1], recv_sem=g_recv.at[d - 1],
            device_id=(sec, req, lax.rem(tp + d, TP)), device_id_type=MESH)

    for d in range(1, TP):
        x_copy(d).start()
        g_copy(d).start()
    xf[tp] = hid[...]
    gfull[tp] = gsend[...]
    for s in range(S):
        @pl.when(s >= sec)
        def _():
            gb[:, s * slot:(s + 1) * slot, :] = jnp.zeros((TP, slot, half), BF)

    def fwd_copy(s, o, d):
        span = pl.ds(s * slot, slot)
        return pltpu.make_async_remote_copy(
            src_ref=gb.at[tp, span], dst_ref=gb.at[tp, span],
            send_sem=f_send.at[o - 1, d - 1], recv_sem=f_recv.at[o - 1, d - 1],
            device_id=(sec, req, lax.rem(tp + d, TP)), device_id_type=MESH)

    q_copy.wait()
    for t in range(T):
        for j in range(HG):
            qs[t, :, j, :] = qv[t, :, j * HEAD:(j + 1) * HEAD].astype(F32)

    for d in range(1, S):
        @pl.when(sec - d >= 0)
        def _():
            s = lax.rem(sec - d + S, S)
            sec_copy(d, s, lax.rem(sec + d, S)).wait_recv()
            for e in range(1, TP):
                fwd_copy(s, d, e).start()

    for c in c_copies:
        c.wait()
    scale = HEAD ** -0.5
    RB = 2

    def old(i, _):
        for b in range(RB):
            r = i * RB + b
            seen = iota((T * G, C), 1) < lens[r]
            for h in range(nt):
                hs = slice(h * G, (h + 1) * G)
                cs = slice(h * HEAD, (h + 1) * HEAD)
                qh = jnp.concatenate([qs[t, r, hs, :] for t in range(T)], axis=0).astype(BF)
                s = lax.dot_general(qh, cv[r, 0, :, cs], (((1,), (1,)), ((), ())), preferred_element_type=F32) * scale
                s = jnp.where(seen, s, -1e30)
                m = jnp.max(s, axis=1, keepdims=True)
                p = jnp.exp(s - m)
                l = jnp.broadcast_to(jnp.sum(p, axis=1, keepdims=True), (T * G, HEAD))
                m = jnp.broadcast_to(m, (T * G, HEAD))
                o = jnp.dot(p.astype(BF), cv[r, 1, :, cs], preferred_element_type=F32)
                for t in range(T):
                    g = slice(t * G, (t + 1) * G)
                    os[t, r, hs, :] = o[g]
                    ms[t, r, hs, :] = m[g]
                    ls[t, r, hs, :] = l[g]
        return 0

    lax.fori_loop(0, R // RB, old, 0)

    lane = iota((M, HEAD), 1)
    exponent = lax.rem(lane, HEAD // 2).astype(F32) * (2.0 / HEAD)
    angle = pos[...].astype(F32) * jnp.exp(exponent * (-math.log(ROPE_BASE)))
    cosine = jnp.cos(angle)
    sine = jnp.where(lane < HEAD // 2, -1.0, 1.0) * jnp.sin(angle)

    for d in range(1, TP):
        x_copy(d).wait_recv()
        g_copy(d).wait_recv()
    for d in range(1, S):
        @pl.when(sec - d >= 0)
        def _():
            for e in range(1, TP):
                fwd_copy(lax.rem(sec - d + S, S), d, e).wait_recv()

    want = ec * slot + (iota((M, 1), 0) // R) * EXIT_CAP + rank_col
    skipped = ec < sec
    W = min(half, 512)
    total = jnp.zeros((M, HEAD), F32)
    for f in range(2):
        choose = (iota((M, S * slot), 1) == want + f * rows).astype(F32).astype(BF)
        for p in range(TP):
            def part(i, total, f=f, p=p, choose=choose):
                gc = pl.ds(pl.multiple_of(i * W, W), W)
                xc = pl.ds(pl.multiple_of(f * half + i * W, W), W)
                came = jnp.dot(choose, gb[p, :, gc], preferred_element_type=F32)
                src = jnp.where(skipped, came, xf[p, :, :, xc].reshape(M, W).astype(F32))
                xf[p, :, :, xc] = src.astype(BF).reshape(T, R, W)
                for k in range(W // HEAD):
                    v = src[:, k * HEAD:(k + 1) * HEAD]
                    total = total + v * v
                return total
            total = lax.fori_loop(0, half // W, part, total)
    inverse = lax.rsqrt(jnp.sum(total, axis=1, keepdims=True) / D + EPSILON)

    er_, ec_ = iota((HEAD, 2 * HEAD), 0), iota((HEAD, 2 * HEAD), 1)
    even = (ec_ == 2 * er_).astype(F32).astype(BF)
    odd = (ec_ == 2 * er_ + 1).astype(F32).astype(BF)
    B = 8
    for p in range(TP):
        def expand(i, _, p=p):
            parts = []
            for b in range(B):
                cols = pl.ds(pl.multiple_of((i * B + b) * HEAD, HEAD), HEAD)
                v = xf[p, :, :, cols].reshape(M, HEAD).astype(F32) * inverse * gfull[p, 0:1, cols]
                parts.append(v.astype(BF))
            x = jnp.concatenate(parts, axis=0)
            a = jnp.dot(x, even, preferred_element_type=F32).astype(BF)
            c = jnp.dot(x, odd, preferred_element_type=F32).astype(BF)
            for b in range(B):
                cols = pl.ds(pl.multiple_of((p * (Dl // HEAD) + i * B + b) * 2 * HEAD, 2 * HEAD), 2 * HEAD)
                lk[0:M, cols] = a[b * M:(b + 1) * M]
                lk[M:2 * M, cols] = c[b * M:(b + 1) * M]
            return 0
        lax.fori_loop(0, Dl // HEAD // B, expand, 0)

    wf = wv.reshape(nt, 2 * D, HEAD)
    acc[...] = jnp.zeros_like(acc)
    KB = 1024
    for c in range(CHUNKS):
        for n in range(nt):
            w_copy(c, n).wait()

        def mm(i, _, c=c):
            k = pl.ds(pl.multiple_of(c * 2 * cd + i * KB, KB), KB)
            rhs = jnp.concatenate([wf[n, k, :] for n in range(nt)], axis=1)
            acc[...] += jnp.dot(lk[:, k], rhs, preferred_element_type=F32)
            return 0
        lax.fori_loop(0, 2 * cd // KB, mm, 0)

    keys, values = [], []
    for h in range(nt):
        cs = slice(h * HEAD, (h + 1) * HEAD)
        k = acc[0:M, cs]
        k = (k * cosine + pltpu.roll(k, HEAD // 2, 1) * sine).astype(BF)
        v = acc[M:2 * M, cs].astype(BF)
        kvout[:, cs] = k
        kvout[:, N + h * HEAD:N + (h + 1) * HEAD] = v
        keys.append(k)
        values.append(v)

    def tail(t, _):
        i, j = iota((R * G, M), 0), iota((R * G, M), 1)
        seen = (i // G == lax.rem(j, R)) & (j // R <= t)
        for h in range(nt):
            hs = slice(h * G, (h + 1) * G)
            q = qs[t, :, hs, :].reshape(R * G, HEAD).astype(BF)
            s = lax.dot_general(q, keys[h], (((1,), (1,)), ((), ())), preferred_element_type=F32) * scale
            s = jnp.where(seen, s, -1e30)
            mo = ms[t, :, hs, :].reshape(R * G, HEAD)
            m = jnp.maximum(mo, jnp.max(s, axis=1, keepdims=True))
            p = jnp.exp(s - m[:, :M])
            a = jnp.exp(mo - m)
            l = ls[t, :, hs, :].reshape(R * G, HEAD) * a + jnp.sum(p, axis=1, keepdims=True)
            o = os[t, :, hs, :].reshape(R * G, HEAD) * a + jnp.dot(p.astype(BF), values[h], preferred_element_type=F32)
            os[t, :, hs, :] = (o / l).reshape(R, G, HEAD)
        return 0

    lax.fori_loop(0, T, tail, 0)
    for t in range(T):
        live = (ec[t * R:(t + 1) * R] > sec).astype(F32)
        for j in range(HG):
            out[t, :, j * HEAD:(j + 1) * HEAD] = (os[t, :, j, :] * live).astype(BF)

    for d in range(1, S):
        @pl.when(sec + d < S)
        def _():
            sec_copy(d, sec, lax.rem(sec + d, S)).wait_send()

        @pl.when(sec - d >= 0)
        def _():
            for e in range(1, TP):
                fwd_copy(lax.rem(sec - d + S, S), d, e).wait_send()
    for d in range(1, TP):
        x_copy(d).wait_send()
        g_copy(d).wait_send()


def local(S, TP, hidden, norm_gain, w_kv, queries, cache_kv, exits, lengths):
    T, _, R, Dl = hidden.shape
    _, D, _, N = w_kv.shape
    C = cache_kv.shape[3]
    nt = N // HEAD
    HG = queries.shape[-1] // HEAD
    M = T * R
    slot = 2 * T * EXIT_CAP
    positions = lengths[None, :] + jnp.arange(T, dtype=jnp.int32)[:, None]
    vmem = pl.BlockSpec(memory_space=pltpu.VMEM)
    hbm = pl.BlockSpec(memory_space=pl.ANY)
    dma = pltpu.SemaphoreType.DMA
    attended, fresh = pl.pallas_call(
        functools.partial(kernel, S, TP),
        out_shape=(jax.ShapeDtypeStruct((T, R, HG * HEAD), BF), jax.ShapeDtypeStruct((M, 2 * N), BF)),
        in_specs=[vmem, vmem, hbm, hbm, hbm, vmem, vmem, vmem, pl.BlockSpec(memory_space=pltpu.SMEM)],
        out_specs=(vmem, vmem),
        scratch_shapes=[
            pltpu.VMEM((nt, D, 2, HEAD), BF),
            pltpu.VMEM((R, 2, C, N), BF),
            pltpu.VMEM((T, R, HG * HEAD), BF),
            pltpu.VMEM((T, R, HG, HEAD), F32),
            pltpu.VMEM((T, R, HG, HEAD), F32),
            pltpu.VMEM((T, R, HG, HEAD), F32),
            pltpu.VMEM((T, R, HG, HEAD), F32),
            pltpu.VMEM((TP, T, R, Dl), BF),
            pltpu.VMEM((TP, S * slot, Dl // 2), BF),
            pltpu.VMEM((slot, Dl // 2), BF),
            pltpu.VMEM((8, Dl), F32),
            pltpu.VMEM((TP, 8, Dl), F32),
            pltpu.VMEM((2 * M, 2 * D), BF),
            pltpu.VMEM((2 * M, N), F32),
            dma((CHUNKS, nt)), dma((2,)), dma,
            dma((S - 1,)), dma((S - 1,)),
            dma((TP - 1,)), dma((TP - 1,)), dma((TP - 1,)), dma((TP - 1,)),
            dma((S - 1, TP - 1)), dma((S - 1, TP - 1)),
        ],
        compiler_params=pltpu.CompilerParams(
            collective_id=0, has_side_effects=True, vmem_limit_bytes=56 << 20),
    )(hidden[:, 0], norm_gain, w_kv[0], queries[:, 0], cache_kv[0],
      exits.reshape(M, 1), exits.reshape(1, M), positions.reshape(M, 1), lengths)
    return attended[:, None], fresh.reshape(T, 1, R, 2, N)


def solution(mesh):
    placed = (
        P(None, "section", "req", "tp"),
        P("section", "tp"),
        P("section", None, None, "tp"),
        P(None, "section", "req", "tp"),
        P("section", "req", None, None, "tp"),
        P(None, "req"),
        P("req"),
    )
    return jax.shard_map(
        functools.partial(local, mesh.shape["section"], mesh.shape["tp"]),
        mesh=mesh,
        in_specs=placed,
        out_specs=(P(None, "section", "req", "tp"), P(None, "section", "req", None, "tp")),
        check_vma=False,
    )
```

time: 115 us -> 54.2 us (0.47)
  the two profiles are of different devices: /device:TPU:0 before, /device:TPU:28 now
where the time goes in v1:
time: 54.2 us; the launch traced here: 53.9 us
  Pallas kernels  45.7 us (84%)
  local copies, waits for them, and re-layouts  6.93 us (13%)
  other arithmetic  0.66 us (1%)
  between operations  0.64 us (1%)
    pallas_call x1, Pallas kernels, local(): pl.pallas_call(functools.partial(kernel, S, TP), out_shape=(jax.ShapeDtyp...  45.7 us
    unnamed x1, local copies, waits for them, and re-layouts  1.87 us
    reshape x1, local copies, waits for them, and re-layouts, local(): return (attended[:, None], fresh.reshape(T, 1, R, 2, N))  1.64 us
    reshape x1, local copies, waits for them, and re-layouts, local(): exits.reshape(M, 1)  1.38 us
    reshape x1, local copies, waits for them, and re-layouts, local(): exits.reshape(1, M)  1.33 us

profile of v1, /device:TPU:28, one launch (start us, length us, event | category | flops | bytes accessed | tf_op | source)
XLA Modules:
  0.0 53.9 jit_solution(16213103260637028446)
XLA Ops:
  0.6 1.3 %reshape.38.erow = s32[1,64]{1,0:T(1,128)} reshape(s32[4,16]{1,0:T(4,128)} %param.12) | data formatting | bytes 512 | tf_op jit(solution)/shard_map/reshape | solution.py:318
  2.0 0.7 %iota_add_fusion = s32[4,16]{1,0:T(4,128)S(1)} fusion(s32[16]{0:T(128)} %lens.1), kind=kLoop, calls=%fused_computation | loop fusion | flops 64 | bytes 320 | tf_op jit(solution)/shard_map/add | solution.py:286
  2.6 0.7 %add.27.pos = s32[64,1]{1,0:T(8,128)} reshape(s32[4,16]{1,0:T(4,128)S(1)} %iota_add_fusion) | data formatting | bytes 512 | tf_op jit(solution)/shard_map/add | solution.py:286
  3.3 1.4 %reshape.40.ecol = s32[64,1]{1,0:T(8,128)} reshape(s32[4,16]{1,0:T(4,128)} %param.12) | data formatting | bytes 512 | tf_op jit(solution)/shard_map/reshape | solution.py:318
  4.7 45.7 %shard_map.86 = (bf16[4,16,4096]{2,1,0:T(8,128)(2,1)}, bf16[64,1024]{1,0:T(8,128)(2,1)}) custom-call(bf16[4,16,4096]{2,1,0:T(8,128)(2,1)} %bitcast.10, bf16[1,4096]{1,0:T(2,128)(2,1)} %gain.1, bf16[8192,2,512]{2,1,0:T(2,128)(2,1)} %bitcast.8, bf16[4,16,4096]{2,1,0:T(8,128)(2,1)} %bitcast.11, bf16[16,2,128,512]{3,2,1,0:T(8,128)(2,1)} %bitcast.9, ...), custom_call_target="tpu_custom_call" | custom-call | tf_op jit(solution)/shard_map/pallas_call | solution.py:290
  50.4 1.6 %reshape.39 = bf16[4,1,16,2,512]{4,3,2,0,1:T(2,128)(2,1)} reshape(bf16[64,1024]{1,0:T(8,128)(2,1)} %get-tuple-element.5) | data formatting | bytes 262144 | tf_op jit(solution)/shard_map/reshape | solution.py:319
  52.0 1.9 %copy.14 = bf16[4,1,16,4096]{3,2,1,0:T(8,128)(2,1)} copy(bf16[4,1,16,4096]{3,2,1,0:T(8,128)(2,1)} %bitcast.12) | data formatting | bytes 1048576

commit v2 on v1

--- a/solution.py
+++ b/solution.py
@@ -22,7 +22,7 @@
     return lax.broadcasted_iota(jnp.int32, shape, axis)
 
 
-def kernel(S, TP, hid, gain, w_hbm, q_hbm, c_hbm, ecol, erow, pos, lens,
+def kernel(S, TP, hid, gain, w_hbm, q_hbm, c_hbm, exits, lrow, lens,
            out, kvout,
            wv, cv, qv, qs, os, ms, ls, xf, gb, pack, gsend, gfull, lk, acc,
            wsem, csem, qsem, sec_send, sec_recv, x_send, x_recv, g_send, g_recv, f_send, f_recv):
@@ -63,9 +63,16 @@
         for n in range(nt):
             w_copy(c, n).start()
 
-    ec = ecol[...]
-    er = erow[...]
     ri, rj = iota((M, M), 0), iota((M, M), 1)
+    own = iota((M, R), 1) == lax.rem(iota((M, R), 0), R)
+
+    def column(spread):
+        return jnp.sum(jnp.where(own, spread.astype(F32), 0.0), axis=1, keepdims=True)
+
+    ecf = column(jnp.concatenate([jnp.broadcast_to(exits[t:t + 1, :], (R, R)) for t in range(T)], axis=0))
+    ec = ecf.astype(jnp.int32)
+    er = jnp.sum(jnp.where(ri == rj, ecf, 0.0), axis=0, keepdims=True).astype(jnp.int32)
+    pos = column(jnp.broadcast_to(lrow[...], (M, R))) + (iota((M, 1), 0) // R).astype(F32)
     same = (ec == er) & (ri // R == rj // R)
     rank_row = jnp.sum((same & (ri < rj)).astype(F32), axis=0, keepdims=True).astype(jnp.int32)
     rank_col = jnp.sum((same & (rj < ri)).astype(F32), axis=1, keepdims=True).astype(jnp.int32)
@@ -131,35 +138,39 @@
     for c in c_copies:
         c.wait()
     scale = HEAD ** -0.5
-    RB = 2
+    RB = 4
+    TG = T * G
 
     def old(i, _):
-        for b in range(RB):
+        pairs = [(b, h) for b in range(RB) for h in range(nt)]
+        scores = []
+        for b, h in pairs:
             r = i * RB + b
-            seen = iota((T * G, C), 1) < lens[r]
-            for h in range(nt):
+            qh = jnp.concatenate([qs[t, r, h * G:(h + 1) * G, :] for t in range(T)], axis=0).astype(BF)
+            s = lax.dot_general(qh, cv[r, 0, :, h * HEAD:(h + 1) * HEAD], (((1,), (1,)), ((), ())), preferred_element_type=F32) * scale
+            scores.append(jnp.where(iota((TG, C), 1) < lens[r], s, -1e30))
+        s = jnp.concatenate(scores, axis=0)
+        m = jnp.max(s, axis=1, keepdims=True)
+        p = jnp.exp(s - m)
+        l = jnp.broadcast_to(jnp.sum(p, axis=1, keepdims=True), (len(pairs) * TG, HEAD))
+        m = jnp.broadcast_to(m, (len(pairs) * TG, HEAD))
+        p = p.astype(BF)
+        for k, (b, h) in enumerate(pairs):
+            r = i * RB + b
+            o = jnp.dot(p[k * TG:(k + 1) * TG], cv[r, 1, :, h * HEAD:(h + 1) * HEAD], preferred_element_type=F32)
+            for t in range(T):
                 hs = slice(h * G, (h + 1) * G)
-                cs = slice(h * HEAD, (h + 1) * HEAD)
-                qh = jnp.concatenate([qs[t, r, hs, :] for t in range(T)], axis=0).astype(BF)
-                s = lax.dot_general(qh, cv[r, 0, :, cs], (((1,), (1,)), ((), ())), preferred_element_type=F32) * scale
-                s = jnp.where(seen, s, -1e30)
-                m = jnp.max(s, axis=1, keepdims=True)
-                p = jnp.exp(s - m)
-                l = jnp.broadcast_to(jnp.sum(p, axis=1, keepdims=True), (T * G, HEAD))
-                m = jnp.broadcast_to(m, (T * G, HEAD))
-                o = jnp.dot(p.astype(BF), cv[r, 1, :, cs], preferred_element_type=F32)
-                for t in range(T):
-                    g = slice(t * G, (t + 1) * G)
-                    os[t, r, hs, :] = o[g]
-                    ms[t, r, hs, :] = m[g]
-                    ls[t, r, hs, :] = l[g]
+                g = slice(k * TG + t * G, k * TG + (t + 1) * G)
+                os[t, r, hs, :] = o[t * G:(t + 1) * G]
+                ms[t, r, hs, :] = m[g]
+                ls[t, r, hs, :] = l[g]
         return 0
 
     lax.fori_loop(0, R // RB, old, 0)
 
     lane = iota((M, HEAD), 1)
     exponent = lax.rem(lane, HEAD // 2).astype(F32) * (2.0 / HEAD)
-    angle = pos[...].astype(F32) * jnp.exp(exponent * (-math.log(ROPE_BASE)))
+    angle = pos * jnp.exp(exponent * (-math.log(ROPE_BASE)))
     cosine = jnp.cos(angle)
     sine = jnp.where(lane < HEAD // 2, -1.0, 1.0) * jnp.sin(angle)
 
@@ -174,7 +185,7 @@
 
     want = ec * slot + (iota((M, 1), 0) // R) * EXIT_CAP + rank_col
     skipped = ec < sec
-    W = min(half, 512)
+    W = min(half, 2048)
     total = jnp.zeros((M, HEAD), F32)
     for f in range(2):
         choose = (iota((M, S * slot), 1) == want + f * rows).astype(F32).astype(BF)
@@ -195,7 +206,7 @@
     er_, ec_ = iota((HEAD, 2 * HEAD), 0), iota((HEAD, 2 * HEAD), 1)
     even = (ec_ == 2 * er_).astype(F32).astype(BF)
     odd = (ec_ == 2 * er_ + 1).astype(F32).astype(BF)
-    B = 8
+    B = min(16, Dl // HEAD)
     for p in range(TP):
         def expand(i, _, p=p):
             parts = []
@@ -215,7 +226,7 @@
 
     wf = wv.reshape(nt, 2 * D, HEAD)
     acc[...] = jnp.zeros_like(acc)
-    KB = 1024
+    KB = 2048
     for c in range(CHUNKS):
         for n in range(nt):
             w_copy(c, n).wait()
@@ -283,14 +294,13 @@
     HG = queries.shape[-1] // HEAD
     M = T * R
     slot = 2 * T * EXIT_CAP
-    positions = lengths[None, :] + jnp.arange(T, dtype=jnp.int32)[:, None]
     vmem = pl.BlockSpec(memory_space=pltpu.VMEM)
     hbm = pl.BlockSpec(memory_space=pl.ANY)
     dma = pltpu.SemaphoreType.DMA
     attended, fresh = pl.pallas_call(
         functools.partial(kernel, S, TP),
         out_shape=(jax.ShapeDtypeStruct((T, R, HG * HEAD), BF), jax.ShapeDtypeStruct((M, 2 * N), BF)),
-        in_specs=[vmem, vmem, hbm, hbm, hbm, vmem, vmem, vmem, pl.BlockSpec(memory_space=pltpu.SMEM)],
+        in_specs=[vmem, vmem, hbm, hbm, hbm, vmem, vmem, pl.BlockSpec(memory_space=pltpu.SMEM)],
         out_specs=(vmem, vmem),
         scratch_shapes=[
             pltpu.VMEM((nt, D, 2, HEAD), BF),
@@ -315,7 +325,7 @@
         compiler_params=pltpu.CompilerParams(
             collective_id=0, has_side_effects=True, vmem_limit_bytes=56 << 20),
     )(hidden[:, 0], norm_gain, w_kv[0], queries[:, 0], cache_kv[0],
-      exits.reshape(M, 1), exits.reshape(1, M), positions.reshape(M, 1), lengths)
+      exits, lengths.reshape(1, R), lengths)
     return attended[:, None], fresh.reshape(T, 1, R, 2, N)
 
 

time: 54.2 us -> 32.1 us (0.59)
  Pallas kernels: 45.7 us -> 27.8 us
  local copies, waits for them, and re-layouts: 6.93 us -> 3.51 us
  other arithmetic: 0.66 us -> 0 us
    pallas_call x1, Pallas kernels: 45.7 us -> 27.8 us  [local(): pl.pallas_call(functools.partial(kernel, S, TP), out_shape=(jax.ShapeDtyp...]
    reshape x2 -> x0, local copies, waits for them, and re-layouts: 2.71 us -> none  [the longest x1 1.38 us: local(): exits.reshape(M, 1)]
    add x1 -> x0, local copies, waits for them, and re-layouts: 0.71 us -> none  [local(): positions = lengths[None, :] + jnp.arange(T, dtype=jnp.int32)[:, None]]
    add x1 -> x0, other arithmetic: 0.66 us -> none  [local(): positions = lengths[None, :] + jnp.arange(T, dtype=jnp.int32)[:, None]]
where the time goes in v2:
time: 32.1 us; the launch traced here: 31.9 us
  Pallas kernels  27.8 us (87%)
  local copies, waits for them, and re-layouts  3.51 us (11%)
  between operations  0.64 us (2%)
    pallas_call x1, Pallas kernels, local(): pl.pallas_call(functools.partial(kernel, S, TP), out_shape=(jax.ShapeDtyp...  27.8 us
    unnamed x1, local copies, waits for them, and re-layouts  1.87 us
    reshape x1, local copies, waits for them, and re-layouts, local(): return (attended[:, None], fresh.reshape(T, 1, R, 2, N))  1.64 us

profile of v2, /device:TPU:28, one launch (start us, length us, event | category | flops | bytes accessed | tf_op | source)
XLA Modules:
  0.0 31.9 jit_solution(18117385505142533442)
XLA Ops:
  0.6 27.8 %shard_map.86 = (bf16[4,16,4096]{2,1,0:T(8,128)(2,1)}, bf16[64,1024]{1,0:T(8,128)(2,1)}) custom-call(bf16[4,16,4096]{2,1,0:T(8,128)(2,1)} %bitcast.11, bf16[1,4096]{1,0:T(2,128)(2,1)} %gain.1, bf16[8192,2,512]{2,1,0:T(2,128)(2,1)} %bitcast.9, bf16[4,16,4096]{2,1,0:T(8,128)(2,1)} %bitcast.12, bf16[16,2,128,512]{3,2,1,0:T(8,128)(2,1)} %bitcast.10, ...), custom_call_target="tpu_custom_call" | custom-call | tf_op jit(solution)/shard_map/pallas_call | solution.py:300
  28.4 1.6 %reshape.11 = bf16[4,1,16,2,512]{4,3,2,0,1:T(2,128)(2,1)} reshape(bf16[64,1024]{1,0:T(8,128)(2,1)} %get-tuple-element.5) | data formatting | bytes 262144 | tf_op jit(solution)/shard_map/reshape | solution.py:329
  30.1 1.9 %copy.12 = bf16[4,1,16,4096]{3,2,1,0:T(8,128)(2,1)} copy(bf16[4,1,16,4096]{3,2,1,0:T(8,128)(2,1)} %bitcast.13) | data formatting | bytes 1048576

commit v3 on v2

--- a/solution.py
+++ b/solution.py
@@ -226,7 +226,7 @@
 
     wf = wv.reshape(nt, 2 * D, HEAD)
     acc[...] = jnp.zeros_like(acc)
-    KB = 2048
+    KB = 2 * cd
     for c in range(CHUNKS):
         for n in range(nt):
             w_copy(c, n).wait()
@@ -250,20 +250,28 @@
         values.append(v)
 
     def tail(t, _):
-        i, j = iota((R * G, M), 0), iota((R * G, M), 1)
-        seen = (i // G == lax.rem(j, R)) & (j // R <= t)
+        RG = R * G
+        i, j = iota((nt * RG, M), 0), iota((nt * RG, M), 1)
+        seen = (lax.rem(i, RG) // G == lax.rem(j, R)) & (j // R <= t)
+
+        def rows_of(ref):
+            return [ref[t, :, h * G:(h + 1) * G, :].reshape(RG, HEAD) for h in range(nt)]
+
+        s = jnp.concatenate([
+            lax.dot_general(q.astype(BF), keys[h], (((1,), (1,)), ((), ())), preferred_element_type=F32)
+            for h, q in enumerate(rows_of(qs))], axis=0) * scale
+        s = jnp.where(seen, s, -1e30)
+        mo = jnp.concatenate(rows_of(ms), axis=0)
+        m = jnp.maximum(mo, jnp.max(s, axis=1, keepdims=True))
+        p = jnp.exp(s - m[:, :M])
+        a = jnp.exp(mo - m)
+        l = jnp.concatenate(rows_of(ls), axis=0) * a + jnp.sum(p, axis=1, keepdims=True)
+        p = p.astype(BF)
+        new = jnp.concatenate([
+            jnp.dot(p[h * RG:(h + 1) * RG], values[h], preferred_element_type=F32) for h in range(nt)], axis=0)
+        o = (jnp.concatenate(rows_of(os), axis=0) * a + new) / l
         for h in range(nt):
-            hs = slice(h * G, (h + 1) * G)
-            q = qs[t, :, hs, :].reshape(R * G, HEAD).astype(BF)
-            s = lax.dot_general(q, keys[h], (((1,), (1,)), ((), ())), preferred_element_type=F32) * scale
-            s = jnp.where(seen, s, -1e30)
-            mo = ms[t, :, hs, :].reshape(R * G, HEAD)
-            m = jnp.maximum(mo, jnp.max(s, axis=1, keepdims=True))
-            p = jnp.exp(s - m[:, :M])
-            a = jnp.exp(mo - m)
-            l = ls[t, :, hs, :].reshape(R * G, HEAD) * a + jnp.sum(p, axis=1, keepdims=True)
-            o = os[t, :, hs, :].reshape(R * G, HEAD) * a + jnp.dot(p.astype(BF), values[h], preferred_element_type=F32)
-            os[t, :, hs, :] = (o / l).reshape(R, G, HEAD)
+            os[t, :, h * G:(h + 1) * G, :] = o[h * RG:(h + 1) * RG].reshape(R, G, HEAD)
         return 0
 
     lax.fori_loop(0, T, tail, 0)

time: 32.1 us -> 30.3 us (0.944)
  Pallas kernels: 27.8 us -> 26 us
    pallas_call x1, Pallas kernels: 27.8 us -> 26 us  [local(): pl.pallas_call(functools.partial(kernel, S, TP), out_shape=(jax.ShapeDtyp...]
where the time goes in v3:
time: 30.3 us; the launch traced here: 30.1 us
  Pallas kernels  26 us (86%)
  local copies, waits for them, and re-layouts  3.51 us (12%)
  between operations  0.64 us (2%)
    pallas_call x1, Pallas kernels, local(): pl.pallas_call(functools.partial(kernel, S, TP), out_shape=(jax.ShapeDtyp...  26 us
    unnamed x1, local copies, waits for them, and re-layouts  1.87 us
    reshape x1, local copies, waits for them, and re-layouts, local(): return (attended[:, None], fresh.reshape(T, 1, R, 2, N))  1.64 us

profile of v3, /device:TPU:28, one launch (start us, length us, event | category | flops | bytes accessed | tf_op | source)
XLA Modules:
  0.0 30.1 jit_solution(13738907783788149269)
XLA Ops:
  0.6 26.0 %shard_map.86 = (bf16[4,16,4096]{2,1,0:T(8,128)(2,1)}, bf16[64,1024]{1,0:T(8,128)(2,1)}) custom-call(bf16[4,16,4096]{2,1,0:T(8,128)(2,1)} %bitcast.11, bf16[1,4096]{1,0:T(2,128)(2,1)} %gain.1, bf16[8192,2,512]{2,1,0:T(2,128)(2,1)} %bitcast.9, bf16[4,16,4096]{2,1,0:T(8,128)(2,1)} %bitcast.12, bf16[16,2,128,512]{3,2,1,0:T(8,128)(2,1)} %bitcast.10, ...), custom_call_target="tpu_custom_call" | custom-call | tf_op jit(solution)/shard_map/pallas_call | solution.py:308
  26.6 1.6 %reshape.11 = bf16[4,1,16,2,512]{4,3,2,0,1:T(2,128)(2,1)} reshape(bf16[64,1024]{1,0:T(8,128)(2,1)} %get-tuple-element.5) | data formatting | bytes 262144 | tf_op jit(solution)/shard_map/reshape | solution.py:337
  28.2 1.9 %copy.12 = bf16[4,1,16,4096]{3,2,1,0:T(8,128)(2,1)} copy(bf16[4,1,16,4096]{3,2,1,0:T(8,128)(2,1)} %bitcast.13) | data formatting | bytes 1048576
